TPU v7x, 32 devices: a whole 2x2x4 slice. The times are simulated.
32 devices in a mesh: grp: 2 (over y), row: 8 (over z, x), sub: 2 (over core).
Axes of the slice: x: 2, y: 2, z: 4, core: 2. Of those that a mesh axis runs over, the one named last changes fastest.
Arguments:
- pair_rep: bfloat16 [64, 32, 128], P(('grp', 'row'), 'sub'), parts along dimension 0, may hold values from -6 to 6
- norm_gain: float32 [128], replicated, may hold values from 0.1 to 1.9
- norm_bias: float32 [128], replicated, may hold values from -3 to 3
- w_a_proj: bfloat16 [128, 128], replicated, may hold values from -0.5 to 0.5
- w_a_gate: bfloat16 [128, 128], replicated, may hold values from -0.5 to 0.5
- w_b_proj: bfloat16 [128, 128], replicated, may hold values from -0.5 to 0.5
- w_b_gate: bfloat16 [128, 128], replicated, may hold values from -0.5 to 0.5
- w_gate: bfloat16 [128, 128], replicated, may hold values from -0.5 to 0.5
- out_gain: float32 [128], replicated, may hold values from 0.1 to 1.9
- out_bias: float32 [128], replicated, may hold values from -3 to 3
- w_out: bfloat16 [128, 128], replicated, may hold values from -0.5 to 0.5
Outputs:
- update: bfloat16 [64, 32, 128], P(('grp', 'row'), 'sub'), parts along dimension 0
There are 2 independent parts, one for each index of `grp`. A program takes and returns all parts, laid end to end along the dimension named above; an argument that names none is the same for every part. Nothing has to cross between parts.
All inputs are finite; a program needn't handle non-finite values.
Results may differ from a plain program's by a relative error of at most 0.012.
Values may be sent and summed in bfloat16 or wider, within the bound.
No kernel may reach another device: no remote copies, remote signals or barrier semaphores. Data moves between devices by JAX's collectives and lax.ppermute only.
A program may use at most 64 MiB of HBM per device.

v0:
```python
import functools

import jax
import jax.numpy as jnp
from jax import lax
from jax.experimental import pallas as pl
from jax.experimental.pallas import tpu as pltpu
from jax.sharding import PartitionSpec as P

EPSILON = 1e-05
GATHER_BYTES = 2 * 1024 * 1024
KERNEL_BYTES = 4 * 1024 * 1024
ROUTES = (
    (3, 14, 4, 9, 5, 11, 0, 8, 1, 10, 7, 15, 2, 12, 6, 13),
    (6, 13, 3, 12, 1, 15, 7, 11, 5, 8, 4, 10, 0, 9, 2, 14),
    (5, 11, 7, 15, 3, 9, 4, 13, 2, 14, 1, 12, 6, 10, 0, 8),
    (1, 9, 0, 11, 7, 13, 2, 15, 6, 12, 3, 8, 4, 14, 5, 10),
)


def layer_norm(values, gain, shift, axis):
    centred = values - jnp.mean(values, axis=axis, keepdims=True)
    variance = jnp.mean(centred * centred, axis=axis, keepdims=True)
    return centred * lax.rsqrt(variance + EPSILON) * gain + shift


def sigmoid(values):
    return 0.5 * jnp.tanh(0.5 * values) + 0.5


def gated(rows, w_proj, w_gate):
    proj = jnp.dot(rows, w_proj, preferred_element_type=jnp.float32)
    gate = jnp.dot(rows, w_gate, preferred_element_type=jnp.float32)
    return sigmoid(gate) * proj


def lookup(values, bits):
    word = sum(value << (bits * place) for place, value in enumerate(values))
    word = jnp.int32(word - (1 << 32) if word >> 31 else word)
    device = lax.axis_index("row") * 2 + lax.axis_index("sub")
    return lax.shift_right_logical(word, device * bits) & ((1 << bits) - 1)


def place_of(sources, span):
    place = lookup([source // 2 % span for source in sources], 2)
    return place, lookup([source % 2 for source in sources], 1)


def copy_kernel(source_ref, target_ref):
    target_ref[...] = source_ref[...]


def flat_normed(values, gain_ref, bias_ref):
    flat = values.reshape(-1, values.shape[-1]).astype(jnp.float32)
    return layer_norm(flat, gain_ref[...], bias_ref[...], -1).astype(jnp.bfloat16)


def finish(left_ref, blocks, places, gating_ref, out_gain_ref, out_bias_ref, w_out_ref):
    sums, gates = [], []
    for block, (place, half) in zip(blocks, places):
        left = left_ref[half], left_ref[1 - half]
        for row in range(left_ref.shape[1]):
            products = block[0] * left[0][row] + block[1] * left[1][row]
            sums.append(jnp.sum(products, axis=1))
        gates.append(gating_ref[place])
    triangle = jnp.concatenate(sums, axis=0)
    hidden_normed = layer_norm(triangle, out_gain_ref[...], out_bias_ref[...], -1)
    mixed = jnp.dot(
        hidden_normed.astype(jnp.bfloat16), w_out_ref[...], preferred_element_type=jnp.float32
    )
    return (jnp.concatenate(gates, axis=0) * mixed).reshape(len(gates), -1, mixed.shape[-1])


def first_kernel(
    span,
    routes,
    own_ref,
    other_ref,
    block_ref,
    norm_gain_ref,
    norm_bias_ref,
    w_a_proj_ref,
    w_a_gate_ref,
    w_b_proj_ref,
    w_b_gate_ref,
    w_gate_ref,
    out_gain_ref,
    out_bias_ref,
    w_out_ref,
    left_ref,
    gating_ref,
    update_ref,
):
    rows, cols, width = own_ref.shape
    sub = lax.axis_index("sub")
    own = flat_normed(own_ref[...], norm_gain_ref, norm_bias_ref)
    other = flat_normed(other_ref[...], norm_gain_ref, norm_bias_ref)
    for values, half in ((own, sub), (other, 1 - sub)):
        left = gated(values, w_a_proj_ref[...], w_a_gate_ref[...])
        left_ref[pl.ds(half, 1)] = left.reshape(1, rows, cols, -1)
    gating = sigmoid(jnp.dot(own, w_gate_ref[...], preferred_element_type=jnp.float32))
    gating = gating.reshape(rows, cols, width)
    for place in range(span):
        part = gating[:, place * rows : (place + 1) * rows]
        gating_ref[place] = part.reshape(rows * rows, width)
    right = gated(flat_normed(block_ref[...], norm_gain_ref, norm_bias_ref), w_b_proj_ref[...], w_b_gate_ref[...])
    right = right.reshape(1, 2, rows, cols, -1)
    places = [place_of(routes[0], span)]
    update_ref[...] = finish(left_ref, right, places, gating_ref, out_gain_ref, out_bias_ref, w_out_ref)


def last_kernel(span, routes, *refs):
    block_refs = refs[: span - 1][::-1]
    (
        left_ref,
        gating_ref,
        first_ref,
        norm_gain_ref,
        norm_bias_ref,
        w_b_proj_ref,
        w_b_gate_ref,
        out_gain_ref,
        out_bias_ref,
        w_out_ref,
        update_ref,
        placed_ref,
    ) = refs[span - 1 :]
    _, rows, cols, width = block_refs[0].shape
    right = jnp.stack([ref[...] for ref in block_refs])
    right = gated(flat_normed(right, norm_gain_ref, norm_bias_ref), w_b_proj_ref[...], w_b_gate_ref[...])
    right = right.reshape(span - 1, 2, rows, cols, -1)
    places = [place_of(sources, span) for sources in routes]
    last = finish(left_ref, right, places[1:], gating_ref, out_gain_ref, out_bias_ref, w_out_ref)
    placed_ref[pl.ds(places[0][0], 1)] = first_ref[...]
    for step in range(span - 1):
        placed_ref[pl.ds(places[step + 1][0], 1)] = last[step : step + 1]
    for row in range(rows):
        parts = [placed_ref[place, row * rows : (row + 1) * rows] for place in range(span)]
        update_ref[row] = jnp.concatenate(parts, axis=0).astype(jnp.bfloat16)


def gather_span(
    routes,
    pair_rep,
    norm_gain,
    norm_bias,
    w_a_proj,
    w_a_gate,
    w_b_proj,
    w_b_gate,
    w_gate,
    out_gain,
    out_bias,
    w_out,
):
    span = len(routes)
    block = pair_rep.shape
    rows, _, width = block
    params = pltpu.CompilerParams(vmem_limit_bytes=KERNEL_BYTES)
    cost = pl.CostEstimate(flops=10**8, bytes_accessed=10**6, transcendentals=0)

    def receive(values, sources):
        pairs = [(source, device) for device, source in enumerate(sources)]
        return lax.ppermute(values, ("row", "sub"), pairs)

    other = receive(pair_rep, [device ^ 1 for device in range(4 * span)])
    own = pl.pallas_call(
        copy_kernel,
        out_shape=jax.ShapeDtypeStruct(block, pair_rep.dtype),
        cost_estimate=cost,
        compiler_params=params,
    )(pair_rep)
    pair = jnp.stack([own, other])
    blocks = [receive(pair, sources) for sources in routes]
    norm = (norm_gain[None], norm_bias[None])
    out = (out_gain[None], out_bias[None], w_out)
    left, gating, update = pl.pallas_call(
        functools.partial(first_kernel, span, routes),
        out_shape=(
            jax.ShapeDtypeStruct((2,) + block, jnp.float32),
            jax.ShapeDtypeStruct((span, rows * rows, width), jnp.float32),
            jax.ShapeDtypeStruct((1, rows * rows, width), jnp.float32),
        ),
        cost_estimate=cost,
        compiler_params=params,
    )(own, other, blocks[0], *norm, w_a_proj, w_a_gate, w_b_proj, w_b_gate, w_gate, *out)
    return pl.pallas_call(
        functools.partial(last_kernel, span, routes),
        out_shape=jax.ShapeDtypeStruct(block, pair_rep.dtype),
        scratch_shapes=[pltpu.VMEM((span, rows * rows, width), jnp.float32)],
        compiler_params=params,
    )(*blocks[:0:-1], left, gating, update, *norm, w_b_proj, w_b_gate, *out)


def exchange_channels(
    pair_rep,
    norm_gain,
    norm_bias,
    w_a_proj,
    w_a_gate,
    w_b_proj,
    w_b_gate,
    w_gate,
    out_gain,
    out_bias,
    w_out,
):
    hidden = w_a_proj.shape[1]
    w_inner = jnp.concatenate([w_a_proj, w_a_gate, w_b_proj, w_b_gate], axis=1)
    normed = layer_norm(pair_rep.astype(jnp.float32), norm_gain, norm_bias, -1).astype(jnp.bfloat16)
    inner = jnp.einsum("rkc,cm->mrk", normed, w_inner, preferred_element_type=jnp.float32)
    left_local = (jax.nn.sigmoid(inner[hidden : 2 * hidden]) * inner[:hidden]).astype(jnp.bfloat16)
    right_local = (
        jax.nn.sigmoid(inner[3 * hidden : 4 * hidden]) * inner[2 * hidden : 3 * hidden]
    ).astype(jnp.bfloat16)
    gating = jax.nn.sigmoid(
        jnp.einsum("rkc,cd->rkd", normed, w_gate, preferred_element_type=jnp.float32)
    ).astype(jnp.bfloat16)
    left_chan, right_chan = (
        lax.all_to_all(left_local, "row", split_axis=0, concat_axis=1, tiled=True),
        lax.all_to_all(right_local, "row", split_axis=0, concat_axis=1, tiled=True),
    )
    left_rows = lax.all_to_all(left_chan, "sub", split_axis=1, concat_axis=2, tiled=True)
    triangle = jnp.einsum(
        "hik,hjk->hij",
        left_rows,
        lax.all_gather(right_chan, "sub", axis=2, tiled=True),
        preferred_element_type=jnp.float32,
    ).astype(jnp.bfloat16)
    regrouped = lax.all_to_all(
        lax.all_to_all(triangle, "sub", split_axis=2, concat_axis=1, tiled=True),
        "row",
        split_axis=1,
        concat_axis=0,
        tiled=True,
    )
    hidden_normed = layer_norm(
        regrouped.astype(jnp.float32), out_gain[:, None, None], out_bias[:, None, None], 0
    ).astype(jnp.bfloat16)
    mixed = jnp.einsum("hrj,hc->rjc", hidden_normed, w_out, preferred_element_type=jnp.float32)
    return (gating.astype(jnp.float32) * mixed).astype(jnp.bfloat16)


def solution(mesh):
    n_row, n_sub = mesh.shape["row"], mesh.shape["sub"]

    def per_device(pair_rep, *weights):
        rows, cols, _ = pair_rep.shape
        gathered = n_row * n_sub * pair_rep.size * pair_rep.dtype.itemsize
        routed = (n_row, n_sub) == (8, 2) and cols == n_row // 2 * rows
        if routed and gathered <= GATHER_BYTES:
            return gather_span(ROUTES, pair_rep, *weights)
        return exchange_channels(pair_rep, *weights)

    in_specs = (P(("grp", "row"), "sub", None), P(), P(), P(), P(), P(), P(), P(), P(), P(), P())
    out_specs = P(("grp", "row"), "sub", None)
    return jax.shard_map(
        per_device, mesh=mesh, in_specs=in_specs, out_specs=out_specs, check_vma=False
    )
```

profile of v0, /device:TPU:1, one launch (start us, length us, event | category | flops | bytes accessed | tf_op | source)
XLA Modules:
  0.0 11.8 jit_solution(6721627160842591736)
XLA Ops:
  0.0 0.1 collective-permute-start
  0.1 0.0 copy-start.10
  0.1 0.7 %copy-done.10 = bf16[4,16,128]{2,1,0:T(8,128)(2,1)S(1)} copy-done((bf16[4,16,128]{2,1,0:T(8,128)(2,1)S(1)}, bf16[4,16,128]{2,1,0:T(8,128)(2,1)}, u32[]{:S(2)}) %copy-start.10) | copy-done | bytes 16408
  0.8 0.6 %collective-permute-done.other_ref = bf16[4,16,128]{2,1,0:T(8,128)(2,1)S(1)} collective-permute-done((bf16[4,16,128]{2,1,0:T(8,128)(2,1)}, bf16[4,16,128]{2,1,0:T(8,128)(2,1)S(1)}, u32[]{:S(2)}, u32[]{:S(2)}) %collective-permute-start) | collective-permute-done | bytes 16416 | tf_op jit(solution)/shard_map/ppermute | solution.py:164
  1.4 3.8 %collective-permute-start.4 = (bf16[2,4,16,128]{3,2,1,0:T(8,128)(2,1)S(1)}, bf16[2,4,16,128]{3,2,1,0:T(8,128)(2,1)S(1)}, u32[]{:S(2)}, u32[]{:S(2)}) collective-permute-start(bf16[2,4,16,128]{3,2,1,0:T(8,128)(2,1)S(1)} %pad_maximum_fusion), channel_id=1, source_target_pairs={{3,0},{14,1},{4,2},{9,3},{5,4},{11,5},{0,6},{8,7},{1,8},{10,9},{7,... | collective-permute-start | bytes 98312 | tf_op jit(solution)/shard_map/ppermute | solution.py:164
  5.2 0.4 %collective-permute-start.3 = (bf16[2,4,16,128]{3,2,1,0:T(8,128)(2,1)S(1)}, bf16[2,4,16,128]{3,2,1,0:T(8,128)(2,1)S(1)}, u32[]{:S(2)}, u32[]{:S(2)}) collective-permute-start(bf16[2,4,16,128]{3,2,1,0:T(8,128)(2,1)S(1)} %pad_maximum_fusion), channel_id=1, source_target_pairs={{6,0},{13,1},{3,2},{12,3},{1,4},{15,5},{7,6},{11,7},{5,8},{8,9},{4... | collective-permute-start | bytes 98312 | tf_op jit(solution)/shard_map/ppermute | solution.py:164
  5.5 0.9 %collective-permute-start.2 = (bf16[2,4,16,128]{3,2,1,0:T(8,128)(2,1)S(1)}, bf16[2,4,16,128]{3,2,1,0:T(8,128)(2,1)S(1)}, u32[]{:S(2)}, u32[]{:S(2)}) collective-permute-start(bf16[2,4,16,128]{3,2,1,0:T(8,128)(2,1)S(1)} %pad_maximum_fusion), channel_id=1, source_target_pairs={{5,0},{11,1},{7,2},{15,3},{3,4},{9,5},{4,6},{13,7},{2,8},{14,9},{1... | collective-permute-start | bytes 98312 | tf_op jit(solution)/shard_map/ppermute | solution.py:164
  6.4 1.4 %collective-permute-start.1 = (bf16[2,4,16,128]{3,2,1,0:T(8,128)(2,1)S(1)}, bf16[2,4,16,128]{3,2,1,0:T(8,128)(2,1)S(1)}, u32[]{:S(2)}, u32[]{:S(2)}) collective-permute-start(bf16[2,4,16,128]{3,2,1,0:T(8,128)(2,1)S(1)} %pad_maximum_fusion), channel_id=1, source_target_pairs={{1,0},{9,1},{0,2},{11,3},{7,4},{13,5},{2,6},{15,7},{6,8},{12,9},{3... | collective-permute-start | bytes 98312 | tf_op jit(solution)/shard_map/ppermute | solution.py:164
  7.8 1.2 %collective-permute-done.4.block_ref = bf16[2,4,16,128]{3,2,1,0:T(8,128)(2,1)S(1)} collective-permute-done((bf16[2,4,16,128]{3,2,1,0:T(8,128)(2,1)S(1)}, bf16[2,4,16,128]{3,2,1,0:T(8,128)(2,1)S(1)}, u32[]{:S(2)}, u32[]{:S(2)}) %collective-permute-start.4) | collective-permute-done | bytes 32800 | tf_op jit(solution)/shard_map/ppermute | solution.py:164
  9.0 0.0 copy-done.2
  9.0 0.0 copy-done.7
  9.0 0.0 copy-done.8
  9.0 0.0 copy-done.9
  9.1 0.0 copy-done
  9.1 0.0 copy-done.1
  9.1 0.6 %copy-done.6 = f32[128]{0:T(128)S(1)} copy-done((f32[128]{0:T(128)S(1)}, f32[128]{0:T(128)}, u32[]{:S(2)}) %copy-start.6) | copy-done | bytes 536
  9.7 0.0 copy-done.3
  9.7 0.0 copy-done.4
  9.7 0.0 copy-done.5
  9.7 0.7 %shard_map.110 = (f32[2,4,16,128]{3,2,1,0:T(8,128)S(1)}, f32[4,16,128]{2,1,0:T(8,128)S(1)}, f32[1,16,128]{2,1,0:T(8,128)S(1)}) custom-call(bf16[4,16,128]{2,1,0:T(8,128)(2,1)S(1)} %shard_map.109.own_ref, bf16[4,16,128]{2,1,0:T(8,128)(2,1)S(1)} %collective-permute-done.other_ref, bf16[2,4,16,128]{3,2,1,0:T(8,128)(2,1)S(1)} %collective-permute-done.4.block_ref, ...), custom_call_target="tpu_custom_call" | custom-call | flops 100000000 | bytes 1000000 | tf_op jit(solution)/shard_map/pallas_call | solution.py:177
  10.4 0.0 collective-permute-done.3.refs_2_
  10.4 0.0 collective-permute-done.2.refs_1_
  10.4 0.0 collective-permute-done.1.refs_0_
  10.4 1.3 %shard_map.111 = bf16[4,16,128]{2,1,0:T(8,128)(2,1)} custom-call(bf16[2,4,16,128]{3,2,1,0:T(8,128)(2,1)S(1)} %collective-permute-done.1.refs_0_, bf16[2,4,16,128]{3,2,1,0:T(8,128)(2,1)S(1)} %collective-permute-done.2.refs_1_, bf16[2,4,16,128]{3,2,1,0:T(8,128)(2,1)S(1)} %collective-permute-done.3.refs_2_, f32[2,4,16,128]{3,2,1,0:T(8,128)S(1)} %get-tuple-element.8.refs_3_, ...), custom_call_target="tpu_custom_call" | custom-call | tf_op jit(solution)/shard_map/pallas_call | solution.py:187
  (12 shorter events, 0.0 us)
Async XLA Ops:
  0.0 1.4 %collective-permute-start = (bf16[4,16,128]{2,1,0:T(8,128)(2,1)}, bf16[4,16,128]{2,1,0:T(8,128)(2,1)S(1)}, u32[]{:S(2)}, u32[]{:S(2)}) collective-permute-start(bf16[4,16,128]{2,1,0:T(8,128)(2,1)} %source_ref.1), channel_id=1, source_target_pairs={{1,0},{0,1},{3,2},{2,3},{5,4},{4,5},{7,6},{6,7},{9,8},{8,9},{11,10... | collective-permute-start | bytes 49160 | tf_op jit(solution)/shard_map/ppermute | solution.py:164
  0.1 0.7 %copy-start.10 = (bf16[4,16,128]{2,1,0:T(8,128)(2,1)S(1)}, bf16[4,16,128]{2,1,0:T(8,128)(2,1)}, u32[]{:S(2)}) copy-start(bf16[4,16,128]{2,1,0:T(8,128)(2,1)} %source_ref.1) | copy-start | bytes 49156
  0.8 8.2 %copy-start.2 = (bf16[128,128]{1,0:T(8,128)(2,1)S(1)}, bf16[128,128]{1,0:T(8,128)(2,1)}, u32[]{:S(2)}) copy-start(bf16[128,128]{1,0:T(8,128)(2,1)} %refs_12_.1) | copy-start | bytes 98308
  0.8 8.2 %copy-start.7 = (bf16[128,128]{1,0:T(8,128)(2,1)S(1)}, bf16[128,128]{1,0:T(8,128)(2,1)}, u32[]{:S(2)}) copy-start(bf16[128,128]{1,0:T(8,128)(2,1)} %w_a_proj_ref.1) | copy-start | bytes 98308
  0.8 8.3 %copy-start.8 = (bf16[128,128]{1,0:T(8,128)(2,1)S(1)}, bf16[128,128]{1,0:T(8,128)(2,1)}, u32[]{:S(2)}) copy-start(bf16[128,128]{1,0:T(8,128)(2,1)} %w_a_gate_ref.1) | copy-start | bytes 98308
  0.8 8.3 %copy-start.9 = (bf16[128,128]{1,0:T(8,128)(2,1)S(1)}, bf16[128,128]{1,0:T(8,128)(2,1)}, u32[]{:S(2)}) copy-start(bf16[128,128]{1,0:T(8,128)(2,1)} %w_gate_ref.1) | copy-start | bytes 98308
  1.4 7.7 %copy-start = (bf16[128,128]{1,0:T(8,128)(2,1)S(1)}, bf16[128,128]{1,0:T(8,128)(2,1)}, u32[]{:S(2)}) copy-start(bf16[128,128]{1,0:T(8,128)(2,1)} %refs_8_.1) | copy-start | bytes 98308
  1.4 7.7 %copy-start.1 = (bf16[128,128]{1,0:T(8,128)(2,1)S(1)}, bf16[128,128]{1,0:T(8,128)(2,1)}, u32[]{:S(2)}) copy-start(bf16[128,128]{1,0:T(8,128)(2,1)} %refs_9_.1) | copy-start | bytes 98308
  1.4 7.6 %collective-permute-start.4 = (bf16[2,4,16,128]{3,2,1,0:T(8,128)(2,1)S(1)}, bf16[2,4,16,128]{3,2,1,0:T(8,128)(2,1)S(1)}, u32[]{:S(2)}, u32[]{:S(2)}) collective-permute-start(bf16[2,4,16,128]{3,2,1,0:T(8,128)(2,1)S(1)} %pad_maximum_fusion), channel_id=1, source_target_pairs={{3,0},{14,1},{4,2},{9,3},{5,4},{11,5},{0,6},{8,7},{1,8},{10,9},{7,... | collective-permute-start | bytes 98312 | tf_op jit(solution)/shard_map/ppermute | solution.py:164
  5.2 5.2 %collective-permute-start.3 = (bf16[2,4,16,128]{3,2,1,0:T(8,128)(2,1)S(1)}, bf16[2,4,16,128]{3,2,1,0:T(8,128)(2,1)S(1)}, u32[]{:S(2)}, u32[]{:S(2)}) collective-permute-start(bf16[2,4,16,128]{3,2,1,0:T(8,128)(2,1)S(1)} %pad_maximum_fusion), channel_id=1, source_target_pairs={{6,0},{13,1},{3,2},{12,3},{1,4},{15,5},{7,6},{11,7},{5,8},{8,9},{4... | collective-permute-start | bytes 98312 | tf_op jit(solution)/shard_map/ppermute | solution.py:164
  5.5 4.9 %collective-permute-start.2 = (bf16[2,4,16,128]{3,2,1,0:T(8,128)(2,1)S(1)}, bf16[2,4,16,128]{3,2,1,0:T(8,128)(2,1)S(1)}, u32[]{:S(2)}, u32[]{:S(2)}) collective-permute-start(bf16[2,4,16,128]{3,2,1,0:T(8,128)(2,1)S(1)} %pad_maximum_fusion), channel_id=1, source_target_pairs={{5,0},{11,1},{7,2},{15,3},{3,4},{9,5},{4,6},{13,7},{2,8},{14,9},{1... | collective-permute-start | bytes 98312 | tf_op jit(solution)/shard_map/ppermute | solution.py:164
  6.4 4.0 %collective-permute-start.1 = (bf16[2,4,16,128]{3,2,1,0:T(8,128)(2,1)S(1)}, bf16[2,4,16,128]{3,2,1,0:T(8,128)(2,1)S(1)}, u32[]{:S(2)}, u32[]{:S(2)}) collective-permute-start(bf16[2,4,16,128]{3,2,1,0:T(8,128)(2,1)S(1)} %pad_maximum_fusion), channel_id=1, source_target_pairs={{1,0},{9,1},{0,2},{11,3},{7,4},{13,5},{2,6},{15,7},{6,8},{12,9},{3... | collective-permute-start | bytes 98312 | tf_op jit(solution)/shard_map/ppermute | solution.py:164
  9.0 0.7 %copy-start.6 = (f32[128]{0:T(128)S(1)}, f32[128]{0:T(128)}, u32[]{:S(2)}) copy-start(f32[128]{0:T(128)} %param.20) | copy-start | bytes 1540
  9.0 0.7 %copy-start.3 = (f32[128]{0:T(128)S(1)}, f32[128]{0:T(128)}, u32[]{:S(2)}) copy-start(f32[128]{0:T(128)} %param.12) | copy-start | bytes 1540
  9.0 0.7 %copy-start.4 = (f32[128]{0:T(128)S(1)}, f32[128]{0:T(128)}, u32[]{:S(2)}) copy-start(f32[128]{0:T(128)} %param.13) | copy-start | bytes 1540
  9.0 0.7 %copy-start.5 = (f32[128]{0:T(128)S(1)}, f32[128]{0:T(128)}, u32[]{:S(2)}) copy-start(f32[128]{0:T(128)} %param.19) | copy-start | bytes 1540
where the time goes:
time: 12 us; the launch traced here: 11.8 us
  starting transfers between devices  6.49 us (54%)
  Pallas kernels  2.04 us (17%)
  waiting for transfers between devices  1.78 us (15%)
  local copies, waits for them, and re-layouts  1.38 us (12%)
    ppermute x5, starting transfers between devices, receive(): return lax.ppermute(values, ('row', 'sub'), pairs)  6.49 us
    ppermute x5, waiting for transfers between devices, receive(): return lax.ppermute(values, ('row', 'sub'), pairs)  1.78 us
    unnamed x22, local copies, waits for them, and re-layouts  1.38 us
    pallas_call x1, Pallas kernels, gather_span(): pl.pallas_call(functools.partial(last_kernel, span, routes), out_shape=ja...  1.34 us
    pallas_call x1, Pallas kernels, gather_span(): pl.pallas_call(functools.partial(first_kernel, span, routes), out_shape=(...  0.7 us
  transfers between devices with their start and end apart: 5, of which 2 were waited for; matrix products, arithmetic and copies ran while one was open for 0% of the time, Pallas kernels for 6%

commit v1 on v0

--- a/solution.py
+++ b/solution.py
@@ -55,66 +55,37 @@
     return layer_norm(flat, gain_ref[...], bias_ref[...], -1).astype(jnp.bfloat16)
 
 
-def finish(left_ref, blocks, places, gating_ref, out_gain_ref, out_bias_ref, w_out_ref):
-    sums, gates = [], []
-    for block, (place, half) in zip(blocks, places):
-        left = left_ref[half], left_ref[1 - half]
-        for row in range(left_ref.shape[1]):
-            products = block[0] * left[0][row] + block[1] * left[1][row]
-            sums.append(jnp.sum(products, axis=1))
-        gates.append(gating_ref[place])
-    triangle = jnp.concatenate(sums, axis=0)
-    hidden_normed = layer_norm(triangle, out_gain_ref[...], out_bias_ref[...], -1)
-    mixed = jnp.dot(
-        hidden_normed.astype(jnp.bfloat16), w_out_ref[...], preferred_element_type=jnp.float32
-    )
-    return (jnp.concatenate(gates, axis=0) * mixed).reshape(len(gates), -1, mixed.shape[-1])
-
-
 def first_kernel(
-    span,
-    routes,
     own_ref,
     other_ref,
-    block_ref,
     norm_gain_ref,
     norm_bias_ref,
     w_a_proj_ref,
     w_a_gate_ref,
+    w_gate_ref,
     w_b_proj_ref,
     w_b_gate_ref,
-    w_gate_ref,
     out_gain_ref,
     out_bias_ref,
     w_out_ref,
     left_ref,
     gating_ref,
-    update_ref,
 ):
-    rows, cols, width = own_ref.shape
+    rows, cols, _ = own_ref.shape
     sub = lax.axis_index("sub")
     own = flat_normed(own_ref[...], norm_gain_ref, norm_bias_ref)
     other = flat_normed(other_ref[...], norm_gain_ref, norm_bias_ref)
     for values, half in ((own, sub), (other, 1 - sub)):
         left = gated(values, w_a_proj_ref[...], w_a_gate_ref[...])
         left_ref[pl.ds(half, 1)] = left.reshape(1, rows, cols, -1)
-    gating = sigmoid(jnp.dot(own, w_gate_ref[...], preferred_element_type=jnp.float32))
-    gating = gating.reshape(rows, cols, width)
-    for place in range(span):
-        part = gating[:, place * rows : (place + 1) * rows]
-        gating_ref[place] = part.reshape(rows * rows, width)
-    right = gated(flat_normed(block_ref[...], norm_gain_ref, norm_bias_ref), w_b_proj_ref[...], w_b_gate_ref[...])
-    right = right.reshape(1, 2, rows, cols, -1)
-    places = [place_of(routes[0], span)]
-    update_ref[...] = finish(left_ref, right, places, gating_ref, out_gain_ref, out_bias_ref, w_out_ref)
+    gating_ref[...] = sigmoid(jnp.dot(own, w_gate_ref[...], preferred_element_type=jnp.float32))
 
 
 def last_kernel(span, routes, *refs):
-    block_refs = refs[: span - 1][::-1]
+    block_refs = refs[:span][::-1]
     (
         left_ref,
         gating_ref,
-        first_ref,
         norm_gain_ref,
         norm_bias_ref,
         w_b_proj_ref,
@@ -124,19 +95,24 @@
         w_out_ref,
         update_ref,
         placed_ref,
-    ) = refs[span - 1 :]
-    _, rows, cols, width = block_refs[0].shape
-    right = jnp.stack([ref[...] for ref in block_refs])
-    right = gated(flat_normed(right, norm_gain_ref, norm_bias_ref), w_b_proj_ref[...], w_b_gate_ref[...])
-    right = right.reshape(span - 1, 2, rows, cols, -1)
-    places = [place_of(sources, span) for sources in routes]
-    last = finish(left_ref, right, places[1:], gating_ref, out_gain_ref, out_bias_ref, w_out_ref)
-    placed_ref[pl.ds(places[0][0], 1)] = first_ref[...]
-    for step in range(span - 1):
-        placed_ref[pl.ds(places[step + 1][0], 1)] = last[step : step + 1]
+    ) = refs[span:]
+    _, rows, cols, _ = block_refs[0].shape
+    for sources, ref in zip(routes, block_refs):
+        place, half = place_of(sources, span)
+        placed_ref[pl.ds(half, 1), pl.ds(place, 1)] = ref[0:1][None]
+        placed_ref[pl.ds(1 - half, 1), pl.ds(place, 1)] = ref[1:2][None]
+    right = flat_normed(placed_ref[...], norm_gain_ref, norm_bias_ref)
+    right = gated(right, w_b_proj_ref[...], w_b_gate_ref[...]).reshape(2, span * rows, cols, -1)
+    sums = []
     for row in range(rows):
-        parts = [placed_ref[place, row * rows : (row + 1) * rows] for place in range(span)]
-        update_ref[row] = jnp.concatenate(parts, axis=0).astype(jnp.bfloat16)
+        products = right[0] * left_ref[0, row] + right[1] * left_ref[1, row]
+        sums.append(jnp.sum(products, axis=1))
+    triangle = jnp.concatenate(sums, axis=0)
+    hidden_normed = layer_norm(triangle, out_gain_ref[...], out_bias_ref[...], -1)
+    mixed = jnp.dot(
+        hidden_normed.astype(jnp.bfloat16), w_out_ref[...], preferred_element_type=jnp.float32
+    )
+    update_ref[...] = (gating_ref[...] * mixed).astype(jnp.bfloat16).reshape(update_ref.shape)
 
 
 def gather_span(
@@ -155,7 +131,7 @@
 ):
     span = len(routes)
     block = pair_rep.shape
-    rows, _, width = block
+    rows, cols, width = block
     params = pltpu.CompilerParams(vmem_limit_bytes=KERNEL_BYTES)
     cost = pl.CostEstimate(flops=10**8, bytes_accessed=10**6, transcendentals=0)
 
@@ -173,23 +149,22 @@
     pair = jnp.stack([own, other])
     blocks = [receive(pair, sources) for sources in routes]
     norm = (norm_gain[None], norm_bias[None])
-    out = (out_gain[None], out_bias[None], w_out)
-    left, gating, update = pl.pallas_call(
-        functools.partial(first_kernel, span, routes),
+    tail = (w_b_proj, w_b_gate, out_gain[None], out_bias[None], w_out)
+    left, gating = pl.pallas_call(
+        first_kernel,
         out_shape=(
             jax.ShapeDtypeStruct((2,) + block, jnp.float32),
-            jax.ShapeDtypeStruct((span, rows * rows, width), jnp.float32),
-            jax.ShapeDtypeStruct((1, rows * rows, width), jnp.float32),
+            jax.ShapeDtypeStruct((rows * cols, width), jnp.float32),
         ),
         cost_estimate=cost,
         compiler_params=params,
-    )(own, other, blocks[0], *norm, w_a_proj, w_a_gate, w_b_proj, w_b_gate, w_gate, *out)
+    )(own, other, *norm, w_a_proj, w_a_gate, w_gate, *tail)
     return pl.pallas_call(
         functools.partial(last_kernel, span, routes),
         out_shape=jax.ShapeDtypeStruct(block, pair_rep.dtype),
-        scratch_shapes=[pltpu.VMEM((span, rows * rows, width), jnp.float32)],
+        scratch_shapes=[pltpu.VMEM((2, span) + block, pair_rep.dtype)],
         compiler_params=params,
-    )(*blocks[:0:-1], left, gating, update, *norm, w_b_proj, w_b_gate, *out)
+    )(*blocks[::-1], left, gating, *norm, *tail)
 
 
 def exchange_channels(

time: 12 us -> 11.9 us (level)
  the two profiles are of different devices: /device:TPU:1 before, /device:TPU:7 now
where the time goes in v1:
time: 11.9 us; the launch traced here: 11.7 us
  starting transfers between devices  7.07 us (59%)
  Pallas kernels  1.73 us (15%)
  waiting for transfers between devices  1.39 us (12%)
  local copies, waits for them, and re-layouts  1.38 us (12%)
    ppermute x5, starting transfers between devices, receive(): return lax.ppermute(values, ('row', 'sub'), pairs)  7.07 us
    pallas_call x1, Pallas kernels, gather_span(): pl.pallas_call(functools.partial(last_kernel, span, routes), out_shape=ja...  1.39 us
    ppermute x5, waiting for transfers between devices, receive(): return lax.ppermute(values, ('row', 'sub'), pairs)  1.39 us
    unnamed x22, local copies, waits for them, and re-layouts  1.38 us
    pallas_call x1, Pallas kernels, gather_span(): pl.pallas_call(first_kernel, out_shape=(jax.ShapeDtypeStruct((2,) + block...  0.34 us
  transfers between devices with their start and end apart: 5, of which 2 were waited for; matrix products, arithmetic and copies ran while one was open for 0% of the time, Pallas kernels for 3%

profile of v1, /device:TPU:7, one launch (start us, length us, event | category | flops | bytes accessed | tf_op | source)
XLA Modules:
  0.0 11.7 jit_solution(10295476742167244150)
XLA Ops:
  0.0 0.7 %collective-permute-start = (bf16[4,16,128]{2,1,0:T(8,128)(2,1)}, bf16[4,16,128]{2,1,0:T(8,128)(2,1)S(1)}, u32[]{:S(2)}, u32[]{:S(2)}) collective-permute-start(bf16[4,16,128]{2,1,0:T(8,128)(2,1)} %source_ref.1), channel_id=1, source_target_pairs={{1,0},{0,1},{3,2},{2,3},{5,4},{4,5},{7,6},{6,7},{9,8},{8,9},{11,10... | collective-permute-start | bytes 49160 | tf_op jit(solution)/shard_map/ppermute | solution.py:140
  0.7 0.7 %copy-done.10 = bf16[4,16,128]{2,1,0:T(8,128)(2,1)S(1)} copy-done((bf16[4,16,128]{2,1,0:T(8,128)(2,1)S(1)}, bf16[4,16,128]{2,1,0:T(8,128)(2,1)}, u32[]{:S(2)}) %copy-start.10) | copy-done | bytes 16408
  1.4 0.0 copy-start.2
  1.4 0.3 %collective-permute-done.other_ref = bf16[4,16,128]{2,1,0:T(8,128)(2,1)S(1)} collective-permute-done((bf16[4,16,128]{2,1,0:T(8,128)(2,1)}, bf16[4,16,128]{2,1,0:T(8,128)(2,1)S(1)}, u32[]{:S(2)}, u32[]{:S(2)}) %collective-permute-start) | collective-permute-done | bytes 16416 | tf_op jit(solution)/shard_map/ppermute | solution.py:140
  1.7 0.5 %collective-permute-start.4 = (bf16[2,4,16,128]{3,2,1,0:T(8,128)(2,1)S(1)}, bf16[2,4,16,128]{3,2,1,0:T(8,128)(2,1)S(1)}, u32[]{:S(2)}, u32[]{:S(2)}) collective-permute-start(bf16[2,4,16,128]{3,2,1,0:T(8,128)(2,1)S(1)} %pad_maximum_fusion), channel_id=1, source_target_pairs={{3,0},{14,1},{4,2},{9,3},{5,4},{11,5},{0,6},{8,7},{1,8},{10,9},{7,... | collective-permute-start | bytes 98312 | tf_op jit(solution)/shard_map/ppermute | solution.py:140
  2.3 3.4 %collective-permute-start.3 = (bf16[2,4,16,128]{3,2,1,0:T(8,128)(2,1)S(1)}, bf16[2,4,16,128]{3,2,1,0:T(8,128)(2,1)S(1)}, u32[]{:S(2)}, u32[]{:S(2)}) collective-permute-start(bf16[2,4,16,128]{3,2,1,0:T(8,128)(2,1)S(1)} %pad_maximum_fusion), channel_id=1, source_target_pairs={{6,0},{13,1},{3,2},{12,3},{1,4},{15,5},{7,6},{11,7},{5,8},{8,9},{4... | collective-permute-start | bytes 98312 | tf_op jit(solution)/shard_map/ppermute | solution.py:140
  5.7 0.4 %collective-permute-start.2 = (bf16[2,4,16,128]{3,2,1,0:T(8,128)(2,1)S(1)}, bf16[2,4,16,128]{3,2,1,0:T(8,128)(2,1)S(1)}, u32[]{:S(2)}, u32[]{:S(2)}) collective-permute-start(bf16[2,4,16,128]{3,2,1,0:T(8,128)(2,1)S(1)} %pad_maximum_fusion), channel_id=1, source_target_pairs={{5,0},{11,1},{7,2},{15,3},{3,4},{9,5},{4,6},{13,7},{2,8},{14,9},{1... | collective-permute-start | bytes 98312 | tf_op jit(solution)/shard_map/ppermute | solution.py:140
  6.1 2.0 %collective-permute-start.1 = (bf16[2,4,16,128]{3,2,1,0:T(8,128)(2,1)S(1)}, bf16[2,4,16,128]{3,2,1,0:T(8,128)(2,1)S(1)}, u32[]{:S(2)}, u32[]{:S(2)}) collective-permute-start(bf16[2,4,16,128]{3,2,1,0:T(8,128)(2,1)S(1)} %pad_maximum_fusion), channel_id=1, source_target_pairs={{1,0},{9,1},{0,2},{11,3},{7,4},{13,5},{2,6},{15,7},{6,8},{12,9},{3... | collective-permute-start | bytes 98312 | tf_op jit(solution)/shard_map/ppermute | solution.py:140
  8.2 0.0 copy-done.2
  8.2 0.0 copy-done.7
  8.2 0.0 copy-done.8
  8.2 0.0 copy-done.9
  8.2 0.0 copy-done
  8.2 0.0 copy-done.1
  8.2 0.6 %copy-done.6 = f32[128]{0:T(128)S(1)} copy-done((f32[128]{0:T(128)S(1)}, f32[128]{0:T(128)}, u32[]{:S(2)}) %copy-start.6) | copy-done | bytes 536
  8.8 0.0 copy-done.3
  8.8 0.0 copy-done.4
  8.8 0.0 copy-done.5
  8.8 0.3 %shard_map.110 = (f32[2,4,16,128]{3,2,1,0:T(8,128)S(1)}, f32[64,128]{1,0:T(8,128)S(1)}) custom-call(bf16[4,16,128]{2,1,0:T(8,128)(2,1)S(1)} %shard_map.109.own_ref, bf16[4,16,128]{2,1,0:T(8,128)(2,1)S(1)} %collective-permute-done.other_ref, f32[1,128]{1,0:T(1,128)S(1)} %bitcast.8, f32[1,128]{1,0:T(1,128)S(1)} %bitcast.10, bf16[128,128]{1,0:T(8,128)(2,1)S(1)} %copy-done.7, ...), custom_call_target="tpu_custom_call" | custom-call | flops 100000000 | bytes 1000000 | tf_op jit(solution)/shard_map/pallas_call | solution.py:153
  9.2 0.0 collective-permute-done.4.refs_3_
  9.2 0.0 collective-permute-done.3.refs_2_
  9.2 1.1 %collective-permute-done.2.refs_1_ = bf16[2,4,16,128]{3,2,1,0:T(8,128)(2,1)S(1)} collective-permute-done((bf16[2,4,16,128]{3,2,1,0:T(8,128)(2,1)S(1)}, bf16[2,4,16,128]{3,2,1,0:T(8,128)(2,1)S(1)}, u32[]{:S(2)}, u32[]{:S(2)}) %collective-permute-start.2) | collective-permute-done | bytes 32800 | tf_op jit(solution)/shard_map/ppermute | solution.py:140
  10.3 0.0 collective-permute-done.1.refs_0_
  10.3 1.4 %shard_map.111 = bf16[4,16,128]{2,1,0:T(8,128)(2,1)} custom-call(bf16[2,4,16,128]{3,2,1,0:T(8,128)(2,1)S(1)} %collective-permute-done.1.refs_0_, bf16[2,4,16,128]{3,2,1,0:T(8,128)(2,1)S(1)} %collective-permute-done.2.refs_1_, bf16[2,4,16,128]{3,2,1,0:T(8,128)(2,1)S(1)} %collective-permute-done.3.refs_2_, ...), custom_call_target="tpu_custom_call" | custom-call | tf_op jit(solution)/shard_map/pallas_call | solution.py:162
  (12 shorter events, 0.0 us)
Async XLA Ops:
  0.0 1.7 %collective-permute-start = (bf16[4,16,128]{2,1,0:T(8,128)(2,1)}, bf16[4,16,128]{2,1,0:T(8,128)(2,1)S(1)}, u32[]{:S(2)}, u32[]{:S(2)}) collective-permute-start(bf16[4,16,128]{2,1,0:T(8,128)(2,1)} %source_ref.1), channel_id=1, source_target_pairs={{1,0},{0,1},{3,2},{2,3},{5,4},{4,5},{7,6},{6,7},{9,8},{8,9},{11,10... | collective-permute-start | bytes 49160 | tf_op jit(solution)/shard_map/ppermute | solution.py:140
  0.7 0.7 %copy-start.10 = (bf16[4,16,128]{2,1,0:T(8,128)(2,1)S(1)}, bf16[4,16,128]{2,1,0:T(8,128)(2,1)}, u32[]{:S(2)}) copy-start(bf16[4,16,128]{2,1,0:T(8,128)(2,1)} %source_ref.1) | copy-start | bytes 49156
  1.4 6.8 %copy-start.2 = (bf16[128,128]{1,0:T(8,128)(2,1)S(1)}, bf16[128,128]{1,0:T(8,128)(2,1)}, u32[]{:S(2)}) copy-start(bf16[128,128]{1,0:T(8,128)(2,1)} %refs_12_.1) | copy-start | bytes 98308
  1.4 6.8 %copy-start.7 = (bf16[128,128]{1,0:T(8,128)(2,1)S(1)}, bf16[128,128]{1,0:T(8,128)(2,1)}, u32[]{:S(2)}) copy-start(bf16[128,128]{1,0:T(8,128)(2,1)} %w_a_proj_ref.1) | copy-start | bytes 98308
  1.4 6.8 %copy-start.8 = (bf16[128,128]{1,0:T(8,128)(2,1)S(1)}, bf16[128,128]{1,0:T(8,128)(2,1)}, u32[]{:S(2)}) copy-start(bf16[128,128]{1,0:T(8,128)(2,1)} %w_a_gate_ref.1) | copy-start | bytes 98308
  1.4 6.8 %copy-start.9 = (bf16[128,128]{1,0:T(8,128)(2,1)S(1)}, bf16[128,128]{1,0:T(8,128)(2,1)}, u32[]{:S(2)}) copy-start(bf16[128,128]{1,0:T(8,128)(2,1)} %w_gate_ref.1) | copy-start | bytes 98308
  1.7 6.5 %copy-start = (bf16[128,128]{1,0:T(8,128)(2,1)S(1)}, bf16[128,128]{1,0:T(8,128)(2,1)}, u32[]{:S(2)}) copy-start(bf16[128,128]{1,0:T(8,128)(2,1)} %refs_8_.1) | copy-start | bytes 98308
  1.7 6.5 %copy-start.1 = (bf16[128,128]{1,0:T(8,128)(2,1)S(1)}, bf16[128,128]{1,0:T(8,128)(2,1)}, u32[]{:S(2)}) copy-start(bf16[128,128]{1,0:T(8,128)(2,1)} %refs_9_.1) | copy-start | bytes 98308
  1.7 7.5 %collective-permute-start.4 = (bf16[2,4,16,128]{3,2,1,0:T(8,128)(2,1)S(1)}, bf16[2,4,16,128]{3,2,1,0:T(8,128)(2,1)S(1)}, u32[]{:S(2)}, u32[]{:S(2)}) collective-permute-start(bf16[2,4,16,128]{3,2,1,0:T(8,128)(2,1)S(1)} %pad_maximum_fusion), channel_id=1, source_target_pairs={{3,0},{14,1},{4,2},{9,3},{5,4},{11,5},{0,6},{8,7},{1,8},{10,9},{7,... | collective-permute-start | bytes 98312 | tf_op jit(solution)/shard_map/ppermute | solution.py:140
  2.3 6.9 %collective-permute-start.3 = (bf16[2,4,16,128]{3,2,1,0:T(8,128)(2,1)S(1)}, bf16[2,4,16,128]{3,2,1,0:T(8,128)(2,1)S(1)}, u32[]{:S(2)}, u32[]{:S(2)}) collective-permute-start(bf16[2,4,16,128]{3,2,1,0:T(8,128)(2,1)S(1)} %pad_maximum_fusion), channel_id=1, source_target_pairs={{6,0},{13,1},{3,2},{12,3},{1,4},{15,5},{7,6},{11,7},{5,8},{8,9},{4... | collective-permute-start | bytes 98312 | tf_op jit(solution)/shard_map/ppermute | solution.py:140
  5.7 4.6 %collective-permute-start.2 = (bf16[2,4,16,128]{3,2,1,0:T(8,128)(2,1)S(1)}, bf16[2,4,16,128]{3,2,1,0:T(8,128)(2,1)S(1)}, u32[]{:S(2)}, u32[]{:S(2)}) collective-permute-start(bf16[2,4,16,128]{3,2,1,0:T(8,128)(2,1)S(1)} %pad_maximum_fusion), channel_id=1, source_target_pairs={{5,0},{11,1},{7,2},{15,3},{3,4},{9,5},{4,6},{13,7},{2,8},{14,9},{1... | collective-permute-start | bytes 98312 | tf_op jit(solution)/shard_map/ppermute | solution.py:140
  6.1 4.2 %collective-permute-start.1 = (bf16[2,4,16,128]{3,2,1,0:T(8,128)(2,1)S(1)}, bf16[2,4,16,128]{3,2,1,0:T(8,128)(2,1)S(1)}, u32[]{:S(2)}, u32[]{:S(2)}) collective-permute-start(bf16[2,4,16,128]{3,2,1,0:T(8,128)(2,1)S(1)} %pad_maximum_fusion), channel_id=1, source_target_pairs={{1,0},{9,1},{0,2},{11,3},{7,4},{13,5},{2,6},{15,7},{6,8},{12,9},{3... | collective-permute-start | bytes 98312 | tf_op jit(solution)/shard_map/ppermute | solution.py:140
  8.1 0.7 %copy-start.6 = (f32[128]{0:T(128)S(1)}, f32[128]{0:T(128)}, u32[]{:S(2)}) copy-start(f32[128]{0:T(128)} %param.20) | copy-start | bytes 1540
  8.1 0.7 %copy-start.3 = (f32[128]{0:T(128)S(1)}, f32[128]{0:T(128)}, u32[]{:S(2)}) copy-start(f32[128]{0:T(128)} %param.12) | copy-start | bytes 1540
  8.1 0.7 %copy-start.4 = (f32[128]{0:T(128)S(1)}, f32[128]{0:T(128)}, u32[]{:S(2)}) copy-start(f32[128]{0:T(128)} %param.13) | copy-start | bytes 1540
  8.1 0.7 %copy-start.5 = (f32[128]{0:T(128)S(1)}, f32[128]{0:T(128)}, u32[]{:S(2)}) copy-start(f32[128]{0:T(128)} %param.19) | copy-start | bytes 1540

commit v2 on v1

--- a/solution.py
+++ b/solution.py
@@ -10,11 +10,11 @@
 EPSILON = 1e-05
 GATHER_BYTES = 2 * 1024 * 1024
 KERNEL_BYTES = 4 * 1024 * 1024
+FIRST = (14, 15, 9, 8, 10, 11, 13, 12, 4, 5, 6, 7, 1, 0, 2, 3)
 ROUTES = (
-    (3, 14, 4, 9, 5, 11, 0, 8, 1, 10, 7, 15, 2, 12, 6, 13),
-    (6, 13, 3, 12, 1, 15, 7, 11, 5, 8, 4, 10, 0, 9, 2, 14),
-    (5, 11, 7, 15, 3, 9, 4, 13, 2, 14, 1, 12, 6, 10, 0, 8),
-    (1, 9, 0, 11, 7, 13, 2, 15, 6, 12, 3, 8, 4, 14, 5, 10),
+    (2, 13, 7, 15, 0, 8, 1, 11, 3, 10, 4, 9, 5, 14, 6, 12),
+    (7, 11, 4, 13, 3, 15, 2, 8, 0, 12, 1, 14, 6, 9, 5, 10),
+    (5, 9, 1, 11, 6, 13, 4, 14, 7, 15, 3, 12, 2, 10, 0, 8),
 )
 
 
@@ -81,9 +81,13 @@
     gating_ref[...] = sigmoid(jnp.dot(own, w_gate_ref[...], preferred_element_type=jnp.float32))
 
 
-def last_kernel(span, routes, *refs):
-    block_refs = refs[:span][::-1]
+def last_kernel(span, first, routes, *refs):
+    block_refs, refs = refs[: span - 1][::-1], refs[span - 1 :]
     (
+        own_ref,
+        other_ref,
+        near_ref,
+        handed_ref,
         left_ref,
         gating_ref,
         norm_gain_ref,
@@ -95,12 +99,22 @@
         w_out_ref,
         update_ref,
         placed_ref,
-    ) = refs[span:]
-    _, rows, cols, _ = block_refs[0].shape
+    ) = refs
+    rows, cols, _ = own_ref.shape
+
+    def put(place, half, values):
+        placed_ref[pl.ds(half, 1), pl.ds(place, 1)] = values[None, None]
+
+    row, sub = lax.axis_index("row"), lax.axis_index("sub")
+    crossed = row // span != sub
+    place, half = place_of(first, span)
+    place, half = jnp.where(crossed, place, lax.rem(row, span)), jnp.where(crossed, half, sub)
+    put(place, half, jnp.where(crossed, near_ref[...], own_ref[...]))
+    put(place, 1 - half, jnp.where(crossed, handed_ref[...], other_ref[...]))
     for sources, ref in zip(routes, block_refs):
         place, half = place_of(sources, span)
-        placed_ref[pl.ds(half, 1), pl.ds(place, 1)] = ref[0:1][None]
-        placed_ref[pl.ds(1 - half, 1), pl.ds(place, 1)] = ref[1:2][None]
+        put(place, half, ref[0])
+        put(place, 1 - half, ref[1])
     right = flat_normed(placed_ref[...], norm_gain_ref, norm_bias_ref)
     right = gated(right, w_b_proj_ref[...], w_b_gate_ref[...]).reshape(2, span * rows, cols, -1)
     sums = []
@@ -116,6 +130,7 @@
 
 
 def gather_span(
+    first,
     routes,
     pair_rep,
     norm_gain,
@@ -129,7 +144,7 @@
     out_bias,
     w_out,
 ):
-    span = len(routes)
+    span = len(routes) + 1
     block = pair_rep.shape
     rows, cols, width = block
     params = pltpu.CompilerParams(vmem_limit_bytes=KERNEL_BYTES)
@@ -139,7 +154,9 @@
         pairs = [(source, device) for device, source in enumerate(sources)]
         return lax.ppermute(values, ("row", "sub"), pairs)
 
-    other = receive(pair_rep, [device ^ 1 for device in range(4 * span)])
+    swap = [device ^ 1 for device in range(4 * span)]
+    near = receive(pair_rep, first)
+    other = receive(pair_rep, swap)
     own = pl.pallas_call(
         copy_kernel,
         out_shape=jax.ShapeDtypeStruct(block, pair_rep.dtype),
@@ -148,6 +165,7 @@
     )(pair_rep)
     pair = jnp.stack([own, other])
     blocks = [receive(pair, sources) for sources in routes]
+    handed = receive(near, swap)
     norm = (norm_gain[None], norm_bias[None])
     tail = (w_b_proj, w_b_gate, out_gain[None], out_bias[None], w_out)
     left, gating = pl.pallas_call(
@@ -160,11 +178,11 @@
         compiler_params=params,
     )(own, other, *norm, w_a_proj, w_a_gate, w_gate, *tail)
     return pl.pallas_call(
-        functools.partial(last_kernel, span, routes),
+        functools.partial(last_kernel, span, first, routes),
         out_shape=jax.ShapeDtypeStruct(block, pair_rep.dtype),
         scratch_shapes=[pltpu.VMEM((2, span) + block, pair_rep.dtype)],
         compiler_params=params,
-    )(*blocks[::-1], left, gating, *norm, *tail)
+    )(*blocks[::-1], own, other, near, handed, left, gating, *norm, *tail)
 
 
 def exchange_channels(
@@ -224,7 +242,7 @@
         gathered = n_row * n_sub * pair_rep.size * pair_rep.dtype.itemsize
         routed = (n_row, n_sub) == (8, 2) and cols == n_row // 2 * rows
         if routed and gathered <= GATHER_BYTES:
-            return gather_span(ROUTES, pair_rep, *weights)
+            return gather_span(FIRST, ROUTES, pair_rep, *weights)
         return exchange_channels(pair_rep, *weights)
 
     in_specs = (P(("grp", "row"), "sub", None), P(), P(), P(), P(), P(), P(), P(), P(), P(), P())

time: 11.9 us -> 12.4 us (1.042)
  the two profiles are of different devices: /device:TPU:7 before, /device:TPU:1 now
where the time goes in v2:
time: 12.4 us; the launch traced here: 12.1 us
  starting transfers between devices  8.12 us (65%)
  Pallas kernels  1.76 us (14%)
  local copies, waits for them, and re-layouts  1.41 us (11%)
  waiting for transfers between devices  0.71 us (6%)
    ppermute x6, starting transfers between devices, receive(): return lax.ppermute(values, ('row', 'sub'), pairs)  8.12 us
    unnamed x22, local copies, waits for them, and re-layouts  1.41 us
    pallas_call x1, Pallas kernels, gather_span(): pl.pallas_call(functools.partial(last_kernel, span, first, routes), out_s...  1.41 us
    ppermute x6, waiting for transfers between devices, receive(): return lax.ppermute(values, ('row', 'sub'), pairs)  0.71 us
    pallas_call x1, Pallas kernels, gather_span(): pl.pallas_call(first_kernel, out_shape=(jax.ShapeDtypeStruct((2,) + block...  0.34 us
  transfers between devices with their start and end apart: 6, of which 3 were waited for; matrix products, arithmetic and copies ran while one was open for 0% of the time, Pallas kernels for 3%

profile of v2, /device:TPU:1, one launch (start us, length us, event | category | flops | bytes accessed | tf_op | source)
XLA Modules:
  0.0 12.1 jit_solution(15983795516995307709)
XLA Ops:
  0.0 0.1 collective-permute-start
  0.1 4.7 %collective-permute-start.4 = (bf16[4,16,128]{2,1,0:T(8,128)(2,1)}, bf16[4,16,128]{2,1,0:T(8,128)(2,1)S(1)}, u32[]{:S(2)}, u32[]{:S(2)}) collective-permute-start(bf16[4,16,128]{2,1,0:T(8,128)(2,1)} %source_ref.1), channel_id=1, source_target_pairs={{14,0},{15,1},{9,2},{8,3},{10,4},{11,5},{13,6},{12,7},{4,8},{5,9},... | collective-permute-start | bytes 49160 | tf_op jit(solution)/shard_map/ppermute | solution.py:155
  4.7 0.7 %copy-done.10 = bf16[4,16,128]{2,1,0:T(8,128)(2,1)S(1)} copy-done((bf16[4,16,128]{2,1,0:T(8,128)(2,1)S(1)}, bf16[4,16,128]{2,1,0:T(8,128)(2,1)}, u32[]{:S(2)}) %copy-start.10) | copy-done | bytes 16408
  5.5 0.0 collective-permute-done.other_ref.refs_4_
  5.5 0.0 copy-start
  5.5 0.0 copy-start.1
  5.5 0.5 %collective-permute-start.3 = (bf16[2,4,16,128]{3,2,1,0:T(8,128)(2,1)S(1)}, bf16[2,4,16,128]{3,2,1,0:T(8,128)(2,1)S(1)}, u32[]{:S(2)}, u32[]{:S(2)}) collective-permute-start(bf16[2,4,16,128]{3,2,1,0:T(8,128)(2,1)S(1)} %pad_maximum_fusion), channel_id=1, source_target_pairs={{2,0},{13,1},{7,2},{15,3},{0,4},{8,5},{1,6},{11,7},{3,8},{10,9},{4... | collective-permute-start | bytes 98312 | tf_op jit(solution)/shard_map/ppermute | solution.py:155
  6.1 1.0 %collective-permute-start.2 = (bf16[2,4,16,128]{3,2,1,0:T(8,128)(2,1)S(1)}, bf16[2,4,16,128]{3,2,1,0:T(8,128)(2,1)S(1)}, u32[]{:S(2)}, u32[]{:S(2)}) collective-permute-start(bf16[2,4,16,128]{3,2,1,0:T(8,128)(2,1)S(1)} %pad_maximum_fusion), channel_id=1, source_target_pairs={{7,0},{11,1},{4,2},{13,3},{3,4},{15,5},{2,6},{8,7},{0,8},{12,9},{1... | collective-permute-start | bytes 98312 | tf_op jit(solution)/shard_map/ppermute | solution.py:155
  7.0 1.2 %collective-permute-start.1 = (bf16[2,4,16,128]{3,2,1,0:T(8,128)(2,1)S(1)}, bf16[2,4,16,128]{3,2,1,0:T(8,128)(2,1)S(1)}, u32[]{:S(2)}, u32[]{:S(2)}) collective-permute-start(bf16[2,4,16,128]{3,2,1,0:T(8,128)(2,1)S(1)} %pad_maximum_fusion), channel_id=1, source_target_pairs={{5,0},{9,1},{1,2},{11,3},{6,4},{13,5},{4,6},{14,7},{7,8},{15,9},{3... | collective-permute-start | bytes 98312 | tf_op jit(solution)/shard_map/ppermute | solution.py:155
  8.2 0.0 collective-permute-done.4.refs_5_
  8.2 0.7 %collective-permute-start.5 = (bf16[4,16,128]{2,1,0:T(8,128)(2,1)S(1)}, bf16[4,16,128]{2,1,0:T(8,128)(2,1)S(1)}, u32[]{:S(2)}, u32[]{:S(2)}) collective-permute-start(bf16[4,16,128]{2,1,0:T(8,128)(2,1)S(1)} %collective-permute-done.4.refs_5_), channel_id=1, source_target_pairs={{1,0},{0,1},{3,2},{2,3},{5,4},{4,5},{7,6},{6,7},{9,8},{8,9},{11,10... | collective-permute-start | bytes 49160 | tf_op jit(solution)/shard_map/ppermute | solution.py:155
  9.0 0.0 copy-done.2
  9.0 0.0 copy-done.7
  9.0 0.0 copy-done.8
  9.0 0.6 %copy-done.6 = f32[128]{0:T(128)S(1)} copy-done((f32[128]{0:T(128)S(1)}, f32[128]{0:T(128)}, u32[]{:S(2)}) %copy-start.6) | copy-done | bytes 536
  9.6 0.0 copy-done.3
  9.6 0.0 copy-done.4
  9.6 0.0 copy-done.5
  9.7 0.3 %shard_map.110 = (f32[2,4,16,128]{3,2,1,0:T(8,128)S(1)}, f32[64,128]{1,0:T(8,128)S(1)}) custom-call(bf16[4,16,128]{2,1,0:T(8,128)(2,1)S(1)} %shard_map.109.own_ref.refs_3_, bf16[4,16,128]{2,1,0:T(8,128)(2,1)S(1)} %collective-permute-done.other_ref.refs_4_, f32[1,128]{1,0:T(1,128)S(1)} %bitcast.8, f32[1,128]{1,0:T(1,128)S(1)} %bitcast.10, ...), custom_call_target="tpu_custom_call" | custom-call | flops 100000000 | bytes 1000000 | tf_op jit(solution)/shard_map/pallas_call | solution.py:171
  10.0 0.0 collective-permute-done.5.refs_6_
  10.0 0.1 %collective-permute-done.3.refs_2_ = bf16[2,4,16,128]{3,2,1,0:T(8,128)(2,1)S(1)} collective-permute-done((bf16[2,4,16,128]{3,2,1,0:T(8,128)(2,1)S(1)}, bf16[2,4,16,128]{3,2,1,0:T(8,128)(2,1)S(1)}, u32[]{:S(2)}, u32[]{:S(2)}) %collective-permute-start.3) | collective-permute-done | bytes 32800 | tf_op jit(solution)/shard_map/ppermute | solution.py:155
  10.2 0.5 %collective-permute-done.2.refs_1_ = bf16[2,4,16,128]{3,2,1,0:T(8,128)(2,1)S(1)} collective-permute-done((bf16[2,4,16,128]{3,2,1,0:T(8,128)(2,1)S(1)}, bf16[2,4,16,128]{3,2,1,0:T(8,128)(2,1)S(1)}, u32[]{:S(2)}, u32[]{:S(2)}) %collective-permute-start.2) | collective-permute-done | bytes 32800 | tf_op jit(solution)/shard_map/ppermute | solution.py:155
  10.6 0.1 collective-permute-done.1.refs_0_
  10.7 1.4 %shard_map.111 = bf16[4,16,128]{2,1,0:T(8,128)(2,1)} custom-call(bf16[2,4,16,128]{3,2,1,0:T(8,128)(2,1)S(1)} %collective-permute-done.1.refs_0_, bf16[2,4,16,128]{3,2,1,0:T(8,128)(2,1)S(1)} %collective-permute-done.2.refs_1_, bf16[2,4,16,128]{3,2,1,0:T(8,128)(2,1)S(1)} %collective-permute-done.3.refs_2_, bf16[4,16,128]{2,1,0:T(8,128)(2,1)S(1)} %shard_map.109.own_ref.refs_3_, ...), custom_call_target="tpu_custom_call" | custom-call | tf_op jit(solution)/shard_map/pallas_call | solution.py:180
  (14 shorter events, 0.0 us)
Async XLA Ops:
  0.0 5.5 %collective-permute-start = (bf16[4,16,128]{2,1,0:T(8,128)(2,1)}, bf16[4,16,128]{2,1,0:T(8,128)(2,1)S(1)}, u32[]{:S(2)}, u32[]{:S(2)}) collective-permute-start(bf16[4,16,128]{2,1,0:T(8,128)(2,1)} %source_ref.1), channel_id=1, source_target_pairs={{1,0},{0,1},{3,2},{2,3},{5,4},{4,5},{7,6},{6,7},{9,8},{8,9},{11,10... | collective-permute-start | bytes 49160 | tf_op jit(solution)/shard_map/ppermute | solution.py:155
  0.1 8.2 %collective-permute-start.4 = (bf16[4,16,128]{2,1,0:T(8,128)(2,1)}, bf16[4,16,128]{2,1,0:T(8,128)(2,1)S(1)}, u32[]{:S(2)}, u32[]{:S(2)}) collective-permute-start(bf16[4,16,128]{2,1,0:T(8,128)(2,1)} %source_ref.1), channel_id=1, source_target_pairs={{14,0},{15,1},{9,2},{8,3},{10,4},{11,5},{13,6},{12,7},{4,8},{5,9},... | collective-permute-start | bytes 49160 | tf_op jit(solution)/shard_map/ppermute | solution.py:155
  4.7 0.8 %copy-start.10 = (bf16[4,16,128]{2,1,0:T(8,128)(2,1)S(1)}, bf16[4,16,128]{2,1,0:T(8,128)(2,1)}, u32[]{:S(2)}) copy-start(bf16[4,16,128]{2,1,0:T(8,128)(2,1)} %source_ref.1) | copy-start | bytes 49156
  5.5 3.5 %copy-start.2 = (bf16[128,128]{1,0:T(8,128)(2,1)S(1)}, bf16[128,128]{1,0:T(8,128)(2,1)}, u32[]{:S(2)}) copy-start(bf16[128,128]{1,0:T(8,128)(2,1)} %refs_15_.1) | copy-start | bytes 98308
  5.5 3.5 %copy-start.7 = (bf16[128,128]{1,0:T(8,128)(2,1)S(1)}, bf16[128,128]{1,0:T(8,128)(2,1)}, u32[]{:S(2)}) copy-start(bf16[128,128]{1,0:T(8,128)(2,1)} %w_a_proj_ref.1) | copy-start | bytes 98308
  5.5 3.5 %copy-start.8 = (bf16[128,128]{1,0:T(8,128)(2,1)S(1)}, bf16[128,128]{1,0:T(8,128)(2,1)}, u32[]{:S(2)}) copy-start(bf16[128,128]{1,0:T(8,128)(2,1)} %w_a_gate_ref.1) | copy-start | bytes 98308
  5.5 3.5 %copy-start.9 = (bf16[128,128]{1,0:T(8,128)(2,1)S(1)}, bf16[128,128]{1,0:T(8,128)(2,1)}, u32[]{:S(2)}) copy-start(bf16[128,128]{1,0:T(8,128)(2,1)} %w_gate_ref.1) | copy-start | bytes 98308
  5.5 3.5 %copy-start = (bf16[128,128]{1,0:T(8,128)(2,1)S(1)}, bf16[128,128]{1,0:T(8,128)(2,1)}, u32[]{:S(2)}) copy-start(bf16[128,128]{1,0:T(8,128)(2,1)} %refs_11_.1) | copy-start | bytes 98308
  5.5 3.5 %copy-start.1 = (bf16[128,128]{1,0:T(8,128)(2,1)S(1)}, bf16[128,128]{1,0:T(8,128)(2,1)}, u32[]{:S(2)}) copy-start(bf16[128,128]{1,0:T(8,128)(2,1)} %refs_12_.1) | copy-start | bytes 98308
  5.5 4.6 %collective-permute-start.3 = (bf16[2,4,16,128]{3,2,1,0:T(8,128)(2,1)S(1)}, bf16[2,4,16,128]{3,2,1,0:T(8,128)(2,1)S(1)}, u32[]{:S(2)}, u32[]{:S(2)}) collective-permute-start(bf16[2,4,16,128]{3,2,1,0:T(8,128)(2,1)S(1)} %pad_maximum_fusion), channel_id=1, source_target_pairs={{2,0},{13,1},{7,2},{15,3},{0,4},{8,5},{1,6},{11,7},{3,8},{10,9},{4... | collective-permute-start | bytes 98312 | tf_op jit(solution)/shard_map/ppermute | solution.py:155
  6.1 4.6 %collective-permute-start.2 = (bf16[2,4,16,128]{3,2,1,0:T(8,128)(2,1)S(1)}, bf16[2,4,16,128]{3,2,1,0:T(8,128)(2,1)S(1)}, u32[]{:S(2)}, u32[]{:S(2)}) collective-permute-start(bf16[2,4,16,128]{3,2,1,0:T(8,128)(2,1)S(1)} %pad_maximum_fusion), channel_id=1, source_target_pairs={{7,0},{11,1},{4,2},{13,3},{3,4},{15,5},{2,6},{8,7},{0,8},{12,9},{1... | collective-permute-start | bytes 98312 | tf_op jit(solution)/shard_map/ppermute | solution.py:155
  7.0 3.7 %collective-permute-start.1 = (bf16[2,4,16,128]{3,2,1,0:T(8,128)(2,1)S(1)}, bf16[2,4,16,128]{3,2,1,0:T(8,128)(2,1)S(1)}, u32[]{:S(2)}, u32[]{:S(2)}) collective-permute-start(bf16[2,4,16,128]{3,2,1,0:T(8,128)(2,1)S(1)} %pad_maximum_fusion), channel_id=1, source_target_pairs={{5,0},{9,1},{1,2},{11,3},{6,4},{13,5},{4,6},{14,7},{7,8},{15,9},{3... | collective-permute-start | bytes 98312 | tf_op jit(solution)/shard_map/ppermute | solution.py:155
  8.2 1.8 %collective-permute-start.5 = (bf16[4,16,128]{2,1,0:T(8,128)(2,1)S(1)}, bf16[4,16,128]{2,1,0:T(8,128)(2,1)S(1)}, u32[]{:S(2)}, u32[]{:S(2)}) collective-permute-start(bf16[4,16,128]{2,1,0:T(8,128)(2,1)S(1)} %collective-permute-done.4.refs_5_), channel_id=1, source_target_pairs={{1,0},{0,1},{3,2},{2,3},{5,4},{4,5},{7,6},{6,7},{9,8},{8,9},{11,10... | collective-permute-start | bytes 49160 | tf_op jit(solution)/shard_map/ppermute | solution.py:155
  9.0 0.7 %copy-start.6 = (f32[128]{0:T(128)S(1)}, f32[128]{0:T(128)}, u32[]{:S(2)}) copy-start(f32[128]{0:T(128)} %param.20) | copy-start | bytes 1540
  9.0 0.7 %copy-start.3 = (f32[128]{0:T(128)S(1)}, f32[128]{0:T(128)}, u32[]{:S(2)}) copy-start(f32[128]{0:T(128)} %param.12) | copy-start | bytes 1540
  9.0 0.7 %copy-start.4 = (f32[128]{0:T(128)S(1)}, f32[128]{0:T(128)}, u32[]{:S(2)}) copy-start(f32[128]{0:T(128)} %param.13) | copy-start | bytes 1540
  9.0 0.7 %copy-start.5 = (f32[128]{0:T(128)S(1)}, f32[128]{0:T(128)}, u32[]{:S(2)}) copy-start(f32[128]{0:T(128)} %param.19) | copy-start | bytes 1540
